TPU v7x, 32 devices: a whole 2x2x4 slice. The times are simulated.
32 devices in a mesh: walk: 8 (over z, x), elec: 2 (over y), chol: 2 (over core).
Axes of the slice: x: 2, y: 2, z: 4, core: 2. Of those that a mesh axis runs over, the one named last changes fastest.
Arguments:
- green: bfloat16 [8, 1024, 256], P('walk'), may hold values from -6 to 6
- chol_vecs: bfloat16 [16, 256, 1024], P(('walk', 'chol'), 'elec'), may hold values from -0.3125 to 0.3125
Outputs:
- gradient: float32 [8, 1024, 256], P('walk', ('elec', 'chol'))
All inputs are finite; a program needn't handle non-finite values.
Results may differ from a plain program's by a relative error of at most 0.0029.
Values may be sent and summed in bfloat16 or wider, within the bound.
A program may use at most 64 MiB of HBM per device.

v0:
```python
import jax
import jax.numpy as jnp
from jax import lax
from jax.sharding import PartitionSpec as P


def shards(green, chol_vecs):
    walkers, orbitals, electrons = green.shape
    starting = jnp.zeros((walkers, orbitals, electrons), jnp.float32)
    blocks = lax.all_gather(chol_vecs, "walk", axis=0, tiled=True)
    number = blocks.shape[0]
    own_rows = blocks.shape[1]
    intersection = jnp.einsum(
        "gap,wpb->gwab", blocks, green, preferred_element_type=jnp.float32
    ).astype(jnp.bfloat16)
    flattened = intersection.reshape(number * walkers, own_rows, electrons)
    received = lax.all_to_all(flattened, "elec", split_axis=2, concat_axis=1, tiled=True)
    received = received.reshape(number, walkers, electrons, own_rows)
    running = starting - jnp.einsum(
        "gap,gwba->wpb", blocks, received, preferred_element_type=jnp.float32
    )
    return lax.psum_scatter(running, ("elec", "chol"), scatter_dimension=1, tiled=True)


def solution(mesh):
    in_specs = (P("walk", None, None), P(("walk", "chol"), "elec", None))
    out_specs = P("walk", ("elec", "chol"), None)
    return jax.shard_map(shards, mesh=mesh, in_specs=in_specs, out_specs=out_specs, check_vma=False)
```

profile of v0, /device:TPU:0, one launch (start us, length us, event | category | flops | bytes accessed | tf_op | source)
XLA Modules:
  0.0 109.8 jit_solution(10957227828885158505)
XLA Ops:
  6.5 0.0 copy-start
  6.5 0.0 all-gather.2.cloned.1.call-start
  6.5 0.7 all-gather.2.cloned.1.call-update
  7.3 0.0 reduce-scatter.2.cloned.1.call-start
  7.3 54.2 %all-gather.2.cloned.1.call-done = bf16[8,128,1024]{2,1,0:T(8,128)(2,1)} async-done(((bf16[1,128,1024]{2,1,0:T(8,128)(2,1)}), bf16[8,128,1024]{2,1,0:T(8,128)(2,1)}) %all-gather.2.cloned.1.call-update) | async-done | bytes 2097168 | tf_op jit(solution)/shard_map/all_gather | solution.py:10
  61.5 0.0 copy-done
  61.5 2.3 %fusion.2 = bf16[8,128,256]{1,2,0:T(8,128)(2,1)S(1)} fusion(bf16[8,128,1024]{2,1,0:T(8,128)(2,1)} %all-gather.2.cloned.1.call-done, bf16[1,1024,256]{2,1,0:T(8,128)(2,1)S(1)} %copy-done), kind=kOutput, calls=%fused_computation.4 | convolution fusion | flops 537133056 | bytes 3145728 | tf_op jit(solution)/shard_map/gap,wpb->gwab/dot_general | solution.py:13
  63.9 0.3 copy.7
  64.2 9.6 %all_to_all.15 = bf16[8,128,256]{1,0,2:T(8,128)(2,1)S(1)} all-to-all(bf16[8,128,256]{1,0,2:T(8,128)(2,1)S(1)} %copy.7), channel_id=1, replica_groups=mesh['walk'=8,'elec'=2,'chol'=2] {'elec'}, dimensions={2} | all-to-all | bytes 1048576 | tf_op jit(solution)/shard_map/all_to_all | solution.py:17
  73.8 0.4 copy.8
  74.2 3.3 %fusion.1 = f32[1,1024,256]{1,2,0:T(8,128)} fusion(bf16[8,256,128]{2,1,0:T(8,128)(2,1)S(1)} %bitcast.29, bf16[8,128,1024]{2,1,0:T(8,128)(2,1)} %all-gather.2.cloned.1.call-done), kind=kOutput, calls=%fused_computation.2 | convolution fusion | flops 537133056 | bytes 3670016 | tf_op jit(solution)/shard_map/gap,gwba->wpb/dot_general | solution.py:19
  77.5 0.0 reduce-scatter.2.cloned.1.call-update
  77.5 23.6 %reduce-scatter.2.cloned.1.call-done = f32[1,256,256]{1,2,0:T(8,128)} async-done(((f32[1,1024,256]{1,2,0:T(8,128)}), f32[1,256,256]{1,2,0:T(8,128)}) %reduce-scatter.2.cloned.1.call-update) | async-done | bytes 262160 | tf_op jit(solution)/shard_map/reduce_scatter | solution.py:22
  101.1 1.8 %copy.9 = f32[1,256,256]{2,1,0:T(8,128)} copy(f32[1,256,256]{1,2,0:T(8,128)} %reduce-scatter.2.cloned.1.call-done) | data formatting | bytes 524288 | tf_op jit(solution)/shard_map/reduce_scatter | solution.py:22
Async XLA Ops:
  6.5 55.0 %copy-start = (bf16[1,1024,256]{2,1,0:T(8,128)(2,1)S(1)}, bf16[1,1024,256]{2,1,0:T(8,128)(2,1)}, u32[]{:S(2)}) copy-start(bf16[1,1024,256]{2,1,0:T(8,128)(2,1)} %param.2) | copy-start | bytes 1572868
  6.5 55.0 %all-gather.2.cloned.1.call-start = ((), (), s32[]{:S(2)}) async-start(), calls=%async_computation.2 | async-start | bytes 2359296 | tf_op jit(solution)/shard_map/all_gather | solution.py:10
  7.3 93.9 %reduce-scatter.2.cloned.1.call-start = ((), (), s32[]{:S(2)}) async-start(), calls=%async_computation.3 | async-start | bytes 1310720 | tf_op jit(solution)/shard_map/reduce_scatter | solution.py:22
Sparse Core Ops, SparseCore 0:
  9.5 51.9 all-gather.1
  77.6 23.4 reduce-scatter.1
where the time goes:
time: 110 us
  waiting for transfers between devices  78.6 us (71%)
  between operations  13.4 us (12%)
  blocking collectives  9.56 us (9%)
  matrix products  5.65 us (5%)
  local copies, waits for them, and re-layouts  2.52 us (2%)
    all_gather x1, waiting for transfers between devices, shards(): blocks = lax.all_gather(chol_vecs, 'walk', axis=0, tiled=True)  54.2 us
    reduce_scatter x1, waiting for transfers between devices, shards(): lax.psum_scatter(running, ('elec', 'chol'), scatter_dimension=1, tiled=True)  23.6 us
    all_to_all x1, blocking collectives, shards(): lax.all_to_all(flattened, 'elec', split_axis=2, concat_axis=1, tiled=True)  9.56 us
    dot_general x1, matrix products, shards(): jnp.einsum('gap,gwba->wpb', blocks, received, preferred_element_type=jnp....  3.3 us
    dot_general x1, matrix products, shards(): jnp.einsum('gap,wpb->gwab', blocks, green, preferred_element_type=jnp.flo...  2.34 us
  transfers between devices with their start and end apart: 2, of which 2 were waited for; matrix products, arithmetic and copies ran while one was open for 0% of the time, Pallas kernels for 0%

commit v1 on v0

v1 whole, which is shorter than its diff:
```python
import functools

import jax
import jax.numpy as jnp
from jax import lax
from jax.experimental import pallas as pl
from jax.experimental.pallas import tpu as pltpu
from jax.sharding import PartitionSpec as P

F32 = jnp.float32
BF16 = jnp.bfloat16


def kernel(n, green, own, out, cholesky, greens, parts, sums_in, sums_out,
           l_send, l_recv, g_send, g_recv, s_send, s_recv, own_sem):
    walk, elec, chol = (lax.axis_index(name) for name in ("walk", "elec", "chol"))
    line = n // 2
    z, x = walk // 2, lax.rem(walk, 2)
    rows, orbitals = own.shape
    quarter = orbitals // 4
    sets = cholesky.shape[0]
    to_x, to_elec, to_chol = {"walk": 2 * z + 1 - x}, {"elec": 1 - elec}, {"chol": 1 - chol}

    def at(place):
        return {"walk": 2 * place + x}

    def others(visit):
        @pl.loop(0, 2 * (line - 1))
        def _(event):
            way, k = lax.rem(event, 2), event // 2
            place = jnp.where(way == 0, line - 1 - k, k)
            pl.when(jnp.where(way == 0, place > z, place < z))(lambda: visit(way, place))

    barrier = pltpu.get_barrier_semaphore()

    def greet(device):
        pl.semaphore_signal(barrier, inc=1, device_id=device, device_id_type=pl.DeviceIdType.MESH)

    for device in (to_x, to_elec, to_chol):
        greet(device)
    others(lambda way, place: greet(at(place)))

    def block(x_at, elec_at):
        return cholesky.at[2 * x_at + chol, pl.ds(pl.multiple_of(elec_at * rows, rows), rows)]

    def strip(elec_at):
        return pl.ds(pl.multiple_of((2 * elec_at + chol) * quarter, quarter), quarter)

    mine = pltpu.make_async_copy(own, block(x, elec), own_sem.at[0])
    mine.start()
    home = pltpu.make_async_copy(green, greens.at[z], own_sem.at[1])
    home.start()

    def remote(source, target, send, recv, device):
        return pltpu.make_async_remote_copy(
            src_ref=source, dst_ref=target, send_sem=send, recv_sem=recv,
            device_id=device, device_id_type=pl.DeviceIdType.MESH)

    def move(i, source, target, device):
        return remote(source, target, l_send.at[i], l_recv.at[i], device)

    own_elec = move(0, own, block(x, elec), to_elec)
    own_x = move(1, own, block(x, elec), to_x)
    own_chol = move(2, own, block(x, elec), to_chol)
    elec_x = move(3, block(x, 1 - elec), block(x, 1 - elec), to_x)
    elec_chol = move(4, block(x, 1 - elec), block(x, 1 - elec), to_chol)
    x_chol = move(5, block(1 - x, elec), block(1 - x, elec), to_chol)
    far_chol = move(6, block(1 - x, 1 - elec), block(1 - x, 1 - elec), to_chol)

    def launch(place):
        return remote(green.at[strip(elec)], greens.at[z, strip(elec)],
                      g_send.at[0, place], g_recv.at[0, z], at(place))

    def spread(kind, place):
        region = greens.at[place, strip(1 - elec if kind == 3 else elec)]
        return remote(region, region, g_send.at[kind, place], g_recv.at[kind, place],
                      to_elec if kind == 1 else to_chol)

    def arrival(place):
        region = greens.at[place, strip(elec)]
        return remote(region, region, g_send.at[0, place], g_recv.at[0, place], at(place))

    pl.semaphore_wait(barrier, line + 2)
    own_elec.start()
    own_x.start()
    others(lambda way, place: launch(place).start())
    own_chol.start()

    own_elec.wait_recv()
    elec_x.start()
    elec_chol.start()

    def pass_on(way, place):
        arrival(place).wait_recv()
        spread(1, place).start()
        spread(2, place).start()

    others(pass_on)
    own_x.wait_recv()
    x_chol.start()

    def pass_over(way, place):
        spread(1, place).wait_recv()
        spread(3, place).start()

    elec_x.wait_recv()
    far_chol.start()
    others(pass_over)
    for copy in (own_chol, elec_chol, x_chol, far_chol):
        copy.wait_recv()
    mine.wait()
    home.wait()

    columns = pl.ds(pl.multiple_of((2 * elec + chol) * quarter, quarter), quarter)

    def contribution(place):
        total = None
        for g in range(sets):
            intersection = jnp.dot(cholesky[g], greens[place], preferred_element_type=F32).astype(BF16)
            term = jnp.dot(intersection, cholesky[g, :, columns], preferred_element_type=F32)
            total = term if total is None else total + term
        return total

    def step(way, place):
        return remote(sums_out.at[way, place], sums_in.at[way, place], s_send.at[way, place],
                      s_recv.at[way, place], at(jnp.where(way == 0, z + 1, z - 1)))

    def add(way, place):
        sums = remote(sums_out.at[way, place], sums_in.at[way, place], s_send.at[way, place],
                      s_recv.at[way, place], to_x)
        sums.wait_recv()
        parts[...] += sums_in[way, place].astype(F32)

    def reduce(way, place):
        spread(2, place).wait_recv()
        spread(3, place).wait_recv()
        parts[...] = contribution(place)
        pl.when(jnp.where(way == 0, z > 0, z < line - 1))(lambda: add(way, place))
        sums_out[way, place] = parts[...].astype(BF16)
        step(way, place).start()

    others(reduce)
    parts[...] = contribution(z)
    pl.when(z > 0)(lambda: add(0, z))
    pl.when(z < line - 1)(lambda: add(1, z))
    out[...] = -parts[...].T

    for copy in (own_elec, own_x, own_chol, elec_x, elec_chol, x_chol, far_chol):
        copy.wait_send()

    def finish(way, place):
        launch(place).wait_send()
        for kind in (1, 2, 3):
            spread(kind, place).wait_send()
        step(way, place).wait_send()

    others(finish)


def shards(n, green, chol_vecs):
    orbitals, electrons = green.shape[1:]
    rows = chol_vecs.shape[1]
    line = n // 2
    quarter = orbitals // 4
    hbm = pl.BlockSpec(memory_space=pltpu.HBM)
    dma = pltpu.SemaphoreType.DMA
    gradient = pl.pallas_call(
        functools.partial(kernel, n),
        out_shape=jax.ShapeDtypeStruct((quarter, electrons), F32),
        in_specs=[hbm, hbm],
        out_specs=pl.BlockSpec(memory_space=pltpu.VMEM),
        scratch_shapes=[
            pltpu.VMEM((4, 2 * rows, orbitals), BF16),
            pltpu.VMEM((line, orbitals, electrons), BF16),
            pltpu.VMEM((electrons, quarter), F32),
            pltpu.VMEM((2, line, electrons, quarter), BF16),
            pltpu.VMEM((2, line, electrons, quarter), BF16),
            dma((7,)), dma((7,)),
            dma((4, line)), dma((4, line)),
            dma((2, line)), dma((2, line)),
            dma((2,)),
        ],
        compiler_params=pltpu.CompilerParams(
            collective_id=0, has_side_effects=True, vmem_limit_bytes=48 * 1024 * 1024),
    )(green[0], chol_vecs[0])
    return gradient[None]


def solution(mesh):
    in_specs = (P("walk", None, None), P(("walk", "chol"), "elec", None))
    out_specs = P("walk", ("elec", "chol"), None)
    return jax.shard_map(functools.partial(shards, mesh.shape["walk"]), mesh=mesh,
                         in_specs=in_specs, out_specs=out_specs, check_vma=False)
```

time: 110 us -> 45.6 us (0.41)
  waiting for transfers between devices: 78.6 us -> 0 us
  Pallas kernels: 0 us -> 42.7 us
  between operations: 13.4 us -> 0.01 us
  blocking collectives: 9.56 us -> 0 us
  matrix products: 5.65 us -> 0 us
    all_gather x1 -> x0, waiting for transfers between devices: 54.2 us -> none  [shards(): blocks = lax.all_gather(chol_vecs, 'walk', axis=0, tiled=True)]
    pallas_call x0 -> x1, Pallas kernels: none -> 42.7 us  [shards(): pl.pallas_call(functools.partial(kernel, n), out_shape=jax.ShapeDtypeStru...]
    reduce_scatter x1 -> x0, waiting for transfers between devices: 23.6 us -> none  [shards(): lax.psum_scatter(running, ('elec', 'chol'), scatter_dimension=1, tiled=True)]
    all_to_all x1 -> x0, blocking collectives: 9.56 us -> none  [shards(): lax.all_to_all(flattened, 'elec', split_axis=2, concat_axis=1, tiled=True)]
    dot_general x2 -> x0, matrix products: 5.65 us -> none  [the longest x1 3.3 us: shards(): jnp.einsum('gap,gwba->wpb', blocks, received, preferred_element_type=jnp....]
    unnamed x2 -> x5, local copies, waits for them, and re-layouts: 0.01 us -> 2.7 us
    reduce_scatter x1 -> x0, local copies, waits for them, and re-layouts: 1.79 us -> none  [shards(): lax.psum_scatter(running, ('elec', 'chol'), scatter_dimension=1, tiled=True)]
  transfers between devices with their start and end apart: 2 -> 0, of which waited for: 2 -> 0; matrix products, arithmetic and copies ran while one was open for 0% -> 0% of each run, Pallas kernels for 0% -> 0%
where the time goes in v1:
time: 45.6 us; the launch traced here: 45.4 us
  Pallas kernels  42.7 us (94%)
  local copies, waits for them, and re-layouts  2.7 us (6%)
    pallas_call x1, Pallas kernels, shards(): pl.pallas_call(functools.partial(kernel, n), out_shape=jax.ShapeDtypeStru...  42.7 us
    unnamed x5, local copies, waits for them, and re-layouts  2.7 us

profile of v1, /device:TPU:0, one launch (start us, length us, event | category | flops | bytes accessed | tf_op | source)
XLA Modules:
  0.0 45.4 jit_solution(6025024556354179621)
XLA Ops:
  0.0 0.0 copy-start
  0.0 1.0 %copy-done = bf16[1,1024,256]{2,1,0:T(8,128)(2,1)S(1)} copy-done((bf16[1,1024,256]{2,1,0:T(8,128)(2,1)S(1)}, bf16[1,1024,256]{2,1,0:T(8,128)(2,1)}, u32[]{:S(2)}) %copy-start) | copy-done | bytes 524312
  1.0 0.0 copy-start.1
  1.0 0.9 %copy-done.1 = bf16[1,128,1024]{2,1,0:T(8,128)(2,1)S(1)} copy-done((bf16[1,128,1024]{2,1,0:T(8,128)(2,1)S(1)}, bf16[1,128,1024]{2,1,0:T(8,128)(2,1)}, u32[]{:S(2)}) %copy-start.1) | copy-done | bytes 262168
  2.0 42.7 %shard_map.28 = f32[256,256]{1,0:T(8,128)S(1)} custom-call(bf16[1024,256]{1,0:T(8,128)(2,1)S(1)} %bitcast.4, bf16[128,1024]{1,0:T(8,128)(2,1)S(1)} %bitcast.5), custom_call_target="tpu_custom_call" | custom-call | tf_op jit(solution)/shard_map/pallas_call | solution.py:167
  44.7 0.7 %copy.4 = f32[1,256,256]{2,1,0:T(8,128)} copy(f32[1,256,256]{2,1,0:T(8,128)S(1)} %bitcast.3) | data formatting | bytes 524288
Async XLA Ops:
  0.0 1.0 %copy-start = (bf16[1,1024,256]{2,1,0:T(8,128)(2,1)S(1)}, bf16[1,1024,256]{2,1,0:T(8,128)(2,1)}, u32[]{:S(2)}) copy-start(bf16[1,1024,256]{2,1,0:T(8,128)(2,1)} %param.2) | copy-start | bytes 1572868
  1.0 0.9 %copy-start.1 = (bf16[1,128,1024]{2,1,0:T(8,128)(2,1)S(1)}, bf16[1,128,1024]{2,1,0:T(8,128)(2,1)}, u32[]{:S(2)}) copy-start(bf16[1,128,1024]{2,1,0:T(8,128)(2,1)} %param.3) | copy-start | bytes 786436
